TPU v7x, 32 devices: a whole 2x2x4 slice. The times are simulated.
32 devices in a mesh: groups: 2 (over x), surf: 16 (over z, y, core).
Axes of the slice: x: 2, y: 2, z: 4, core: 2. Of those that a mesh axis runs over, the one named last changes fastest.
Arguments:
- sensitivity: bfloat16 [96, 131072], P(None, ('groups', 'surf')), parts along dimension 1, may hold values from -6 to 6
- owner: int32 [131072], P(('groups', 'surf')), parts along dimension 0, may hold values from 0 to 65535, as said below
- patch_count: int32 [32], P(('groups', 'surf')), parts along dimension 0, may hold values from 16 to 32, as said below
- neighbours: int32 [1024, 9], P(('groups', 'surf')), parts along dimension 0, may hold values from 0 to 511, as said below
- coupling: float32 [1024, 9], P(('groups', 'surf')), parts along dimension 0, may hold values from 0.25 to 2
Outputs:
- surface_grad: float32 [96, 131072], P(None, ('groups', 'surf')), parts along dimension 1
- smoothed: float32 [96, 131072], P(None, ('groups', 'surf')), parts along dimension 1
There are 2 independent parts, one for each index of `groups`. A program takes and returns all parts, laid end to end along the dimension named above; each array names one. Nothing has to cross between parts.
Inputs may be any that keep to these rules, and one draw needn't show every extreme that they name: Each face's owner lies in the node range of its own partition or of a partition beside it, 4096 nodes a partition. `patch_count`: the first partition is full. `neighbours`: each neighbour differs from its patch by 1 to 4 in patch order.
All inputs are finite; a program needn't handle non-finite values.
Results may differ from a plain program's by a relative error of at most 0.0003.
Values may be sent and summed in bfloat16 or wider, within the bound.
A program may use at most 64 MiB of HBM per device.

v0:
```python
import functools

import jax
import jax.numpy as jnp
from jax import lax
from jax.experimental import pallas as pl
from jax.experimental.pallas import tpu as pltpu
from jax.sharding import PartitionSpec as P

NODES = 128
REACH = 4
SWEEPS = 4
LOW = 256
LANES = 128
smoothing = 1.5
OFFSETS = [d for d in range(-REACH, REACH + 1) if d != 0]
NOFF = len(OFFSETS)
MESH = pl.DeviceIdType.MESH


def kernel(
    chunk,
    sens,
    owner,
    count,
    neighbours,
    coupling,
    surface_out,
    smooth_out,
    values,
    owners,
    masked,
    low_hot,
    acc,
    fields,
    weights,
    surface_stage,
    smooth_stage,
    load_sem,
    oload_sem,
    send_sem,
    recv_sem,
    osend_sem,
    orecv_sem,
    hsend_sem,
    hrecv_sem,
    out_sem,
):
    columns, faces = sens.shape
    patches = neighbours.shape[0]
    span = patches * NODES
    highs = span // LOW
    chunks = faces // chunk
    pieces = chunk // LANES
    orow = faces // LANES
    position = lax.axis_index("surf")
    peers = lax.axis_size("surf")
    has_below = position > 0
    has_above = position < peers - 1

    def local_load(k):
        return pltpu.make_async_copy(sens.at[:, pl.ds(k * chunk, chunk)], values.at[0, k], load_sem.at[k])

    def face_copy(side, k):
        target = position + 1 if side == 0 else position - 1
        return pltpu.make_async_remote_copy(
            src_ref=sens.at[:, pl.ds(k * chunk, chunk)],
            dst_ref=values.at[1 + side, k],
            send_sem=send_sem.at[side, k],
            recv_sem=recv_sem.at[side, k],
            device_id={"surf": target},
            device_id_type=MESH,
        )

    def owner_copy(side):
        target = position + 1 if side == 0 else position - 1
        return pltpu.make_async_remote_copy(
            src_ref=owner,
            dst_ref=owners.at[1 + side],
            send_sem=osend_sem.at[side],
            recv_sem=orecv_sem.at[side],
            device_id={"surf": target},
            device_id_type=MESH,
        )

    def halo_copy(side, sweep):
        target = position + 1 if side == 0 else position - 1
        source = patches if side == 0 else REACH
        landing = 0 if side == 0 else patches + REACH
        return pltpu.make_async_remote_copy(
            src_ref=fields.at[sweep, pl.ds(source, REACH)],
            dst_ref=fields.at[sweep, pl.ds(landing, REACH)],
            send_sem=hsend_sem.at[side, sweep],
            recv_sem=hrecv_sem.at[side, sweep],
            device_id={"surf": target},
            device_id_type=MESH,
        )

    own_owner = pltpu.make_async_copy(owner, owners.at[0], oload_sem)
    own_owner.start()
    for k in range(chunks):
        local_load(k).start()

    barrier = pltpu.get_barrier_semaphore()

    @pl.when(has_below)
    def _():
        pl.semaphore_signal(barrier, inc=1, device_id={"surf": position - 1}, device_id_type=MESH)

    @pl.when(has_above)
    def _():
        pl.semaphore_signal(barrier, inc=1, device_id={"surf": position + 1}, device_id_type=MESH)

    both = jnp.logical_and(has_below, has_above)

    @pl.when(both)
    def _():
        pl.semaphore_wait(barrier, 2)

    @pl.when(jnp.logical_not(both))
    def _():
        pl.semaphore_wait(barrier, 1)

    @pl.when(has_above)
    def _():
        owner_copy(0).start()

    @pl.when(has_below)
    def _():
        owner_copy(1).start()

    for k in range(chunks):

        @pl.when(has_above)
        def _(k=k):
            face_copy(0, k).start()

        @pl.when(has_below)
        def _(k=k):
            face_copy(1, k).start()

    slots = lax.broadcasted_iota(jnp.int32, neighbours.shape, 0)
    distance = neighbours[...] - (position * patches + slots)
    links = coupling[...]
    rows = lax.broadcasted_iota(jnp.int32, (patches, LANES), 0)
    alive = jnp.where(rows < count[0], 1.0, 0.0).astype(jnp.float32)
    diagonal = 1.0 + smoothing * (2.0 + jnp.sum(links, axis=1, keepdims=True))
    share = alive / jnp.broadcast_to(diagonal, alive.shape)
    weights[NOFF] = share
    weights[NOFF + 1] = smoothing * share
    weights[NOFF + 2] = alive
    for at, offset in enumerate(OFFSETS):
        total = jnp.sum(jnp.where(distance == offset, links, 0.0), axis=1, keepdims=True)
        weights[at] = smoothing * share * jnp.broadcast_to(total, alive.shape)

    zero_halo = jnp.zeros((REACH, columns, NODES), jnp.float32)

    @pl.when(jnp.logical_not(has_below))
    def _():
        for sweep in range(SWEEPS):
            fields[sweep, pl.ds(0, REACH)] = zero_halo

    @pl.when(jnp.logical_not(has_above))
    def _():
        for sweep in range(SWEEPS):
            fields[sweep, pl.ds(patches + REACH, REACH)] = zero_halo

    acc[...] = jnp.zeros_like(acc)
    first_node = position * span
    low_rows = lax.broadcasted_iota(jnp.int32, (LOW, LANES), 0)

    def add_chunk(slot, k):
        for j in range(pieces):
            local = owners[slot, pl.ds(k * pieces + j, 1), :] - first_node
            high = (local >> 8).astype(jnp.float32).astype(jnp.bfloat16)
            low = local & (LOW - 1)
            lanes = pl.ds(j * LANES, LANES)
            low_hot[:, lanes] = jnp.where(low_rows == low, 1.0, 0.0).astype(jnp.bfloat16)
            vals = values[slot, k, :, lanes]
            high_full = jnp.broadcast_to(high, vals.shape)
            for h in range(highs):
                masked[pl.ds(h * columns, columns), lanes] = jnp.where(
                    high_full == jnp.bfloat16(h), vals, jnp.bfloat16(0)
                )
        acc[...] += lax.dot_general(
            masked[...],
            low_hot[...],
            (((1,), (1,)), ((), ())),
            preferred_element_type=jnp.float32,
        )

    own_owner.wait()

    def step(s, carry):
        is_own = s < chunks
        t = jnp.maximum(s - chunks, 0)
        side = lax.rem(t, 2)
        k = jnp.where(is_own, s, t // 2)
        slot = jnp.where(is_own, 0, 1 + side)

        @pl.when(is_own)
        def _():
            local_load(k).wait()

        from_below = jnp.logical_and(jnp.logical_not(is_own), side == 0)
        from_above = jnp.logical_and(jnp.logical_not(is_own), side == 1)

        @pl.when(jnp.logical_and(from_below, has_below))
        def _():
            @pl.when(t == 0)
            def _():
                owner_copy(0).wait_recv()

            face_copy(0, k).wait_recv()

        @pl.when(jnp.logical_and(from_above, has_above))
        def _():
            @pl.when(t == 1)
            def _():
                owner_copy(1).wait_recv()

            face_copy(1, k).wait_recv()

        present = jnp.logical_or(
            is_own,
            jnp.logical_or(jnp.logical_and(side == 0, has_below), jnp.logical_and(side == 1, has_above)),
        )

        @pl.when(present)
        def _():
            add_chunk(slot, k)

        return carry

    lax.fori_loop(0, 3 * chunks, step, 0)

    def put_surface(h):
        for half in range(LOW // NODES):
            p = h * (LOW // NODES) + half
            patch = acc[pl.ds(h * columns, columns), pl.ds(half * NODES, NODES)]
            patch = patch * weights[NOFF + 2, pl.ds(p, 1), :]
            fields[0, REACH + p] = patch
            surface_stage[:, pl.ds(p * NODES, NODES)] = patch

    def send_halo(sweep):
        @pl.when(has_above)
        def _():
            halo_copy(0, sweep).start()

        @pl.when(has_below)
        def _():
            halo_copy(1, sweep).start()

    def wait_halo(sweep):
        @pl.when(has_below)
        def _():
            halo_copy(0, sweep).wait_recv()

        @pl.when(has_above)
        def _():
            halo_copy(1, sweep).wait_recv()

    ends = REACH * NODES // LOW
    for h in list(range(ends)) + list(range(highs - ends, highs)):
        put_surface(h)
    send_halo(0)
    for h in range(ends, highs - ends):
        put_surface(h)
    surface_copy = pltpu.make_async_copy(surface_stage, surface_out, out_sem.at[0])
    surface_copy.start()

    def relax(sweep, p):
        parts = [weights[at, pl.ds(p, 1), :] for at in range(NOFF + 2)]
        for block in range(columns // 8):
            c = pl.ds(block * 8, 8)
            here = fields[sweep, p + REACH, c, :]
            total = parts[NOFF] * fields[0, p + REACH, c, :]
            total = total + parts[NOFF + 1] * (pltpu.roll(here, 1, 1) + pltpu.roll(here, NODES - 1, 1))
            for at, offset in enumerate(OFFSETS):
                total = total + parts[at] * fields[sweep, p + REACH + offset, c, :]
            if sweep == SWEEPS - 1:
                smooth_stage[c, pl.ds(pl.multiple_of(p * NODES, NODES), NODES)] = total
            else:
                fields[sweep + 1, p + REACH, c, :] = total

    def relax_range(sweep, low, high):
        def one(p, carry):
            relax(sweep, p)
            return carry

        lax.fori_loop(low, high, one, 0)

    for sweep in range(SWEEPS):
        last = sweep == SWEEPS - 1
        if last:
            relax_range(sweep, REACH, patches - REACH)
        wait_halo(sweep)
        relax_range(sweep, 0, REACH)
        relax_range(sweep, patches - REACH, patches)
        if not last:
            send_halo(sweep + 1)
            relax_range(sweep, REACH, patches - REACH)

    smooth_copy = pltpu.make_async_copy(smooth_stage, smooth_out, out_sem.at[1])
    smooth_copy.start()
    surface_copy.wait()
    smooth_copy.wait()

    for side, there in ((0, has_above), (1, has_below)):

        @pl.when(there)
        def _(side=side):
            owner_copy(side).wait_send()
            for k in range(chunks):
                face_copy(side, k).wait_send()
            for sweep in range(SWEEPS):
                halo_copy(side, sweep).wait_send()


def body(sensitivity, owner, patch_count, neighbours, coupling):
    columns, faces = sensitivity.shape
    patches = neighbours.shape[0]
    span = patches * NODES
    chunk = min(1024, faces)
    chunks = faces // chunk
    highs = span // LOW
    any_space = pl.BlockSpec(memory_space=pl.ANY)
    vmem = pl.BlockSpec(memory_space=pltpu.VMEM)
    out = jax.ShapeDtypeStruct((columns, span), jnp.float32)
    dma = pltpu.SemaphoreType.DMA
    return pl.pallas_call(
        functools.partial(kernel, chunk),
        out_shape=(out, out),
        in_specs=[any_space, vmem, pl.BlockSpec(memory_space=pltpu.SMEM), vmem, vmem],
        out_specs=(any_space, any_space),
        scratch_shapes=[
            pltpu.VMEM((3, chunks, columns, chunk), jnp.bfloat16),
            pltpu.VMEM((3, faces // LANES, LANES), jnp.int32),
            pltpu.VMEM((highs * columns, chunk), jnp.bfloat16),
            pltpu.VMEM((LOW, chunk), jnp.bfloat16),
            pltpu.VMEM((highs * columns, LOW), jnp.float32),
            pltpu.VMEM((SWEEPS, patches + 2 * REACH, columns, NODES), jnp.float32),
            pltpu.VMEM((NOFF + 3, patches, LANES), jnp.float32),
            pltpu.VMEM((columns, span), jnp.float32),
            pltpu.VMEM((columns, span), jnp.float32),
            dma((chunks,)),
            dma,
            dma((2, chunks)),
            dma((2, chunks)),
            dma((2,)),
            dma((2,)),
            dma((2, SWEEPS)),
            dma((2, SWEEPS)),
            dma((2,)),
        ],
        compiler_params=pltpu.CompilerParams(
            collective_id=0, has_side_effects=True, vmem_limit_bytes=48 * 1024 * 1024
        ),
    )(sensitivity, owner.reshape(faces // LANES, LANES), patch_count, neighbours, coupling)


def solution(mesh):
    placed = (
        P(None, ("groups", "surf")),
        P(("groups", "surf")),
        P(("groups", "surf")),
        P(("groups", "surf"), None),
        P(("groups", "surf"), None),
    )
    return jax.shard_map(
        body,
        mesh=mesh,
        in_specs=placed,
        out_specs=(P(None, ("groups", "surf")), P(None, ("groups", "surf"))),
        check_vma=False,
    )
```

profile of v0, /device:TPU:17, one launch (start us, length us, event | category | flops | bytes accessed | tf_op | source)
XLA Modules:
  0.0 60.7 jit_solution(17504310965094897844)
XLA Ops:
  1.3 0.8 %copy.7.neighbours = s32[32,9]{1,0:T(8,128)S(1)} copy(s32[32,9]{0,1:T(8,128)} %param.8) | data formatting | bytes 2304 | tf_op args[3]
  2.1 0.8 %copy.8.coupling = f32[32,9]{1,0:T(8,128)S(1)} copy(f32[32,9]{0,1:T(8,128)} %param.9) | data formatting | bytes 2304 | tf_op args[4]
  2.8 0.0 copy-start
  2.8 1.1 %copy-done = bf16[96,4096]{1,0:T(8,128)(2,1)S(1)} copy-done((bf16[96,4096]{1,0:T(8,128)(2,1)S(1)}, bf16[96,4096]{1,0:T(8,128)(2,1)}, u32[]{:S(2)}) %copy-start) | copy-done | bytes 786456
  4.0 0.0 copy-start.1
  4.0 0.7 %copy-done.1 = s32[4096]{0:T(1024)S(1)} copy-done((s32[4096]{0:T(1024)S(1)}, s32[4096]{0:T(1024)}, u32[]{:S(2)}) %copy-start.1) | copy-done | bytes 16408
  4.7 53.7 %shard_map.68 = (f32[96,4096]{1,0:T(8,128)S(1)}, f32[96,4096]{1,0:T(8,128)S(1)}) custom-call(bf16[96,4096]{1,0:T(8,128)(2,1)S(1)} %copy-done, s32[32,128]{1,0:T(8,128)S(1)} %bitcast.1, s32[1]{0:T(128)S(6)} %copy.11.count, s32[32,9]{1,0:T(8,128)S(1)} %copy.7.neighbours, f32[32,9]{1,0:T(8,128)S(1)} %copy.8.coupling), custom_call_target="tpu_custom_call" | custom-call | tf_op jit(solution)/shard_map/pallas_call | solution.py:331
  58.4 1.1 %copy.12 = f32[96,4096]{1,0:T(8,128)} copy(f32[96,4096]{1,0:T(8,128)S(1)} %get-tuple-element.4) | data formatting | bytes 3145728
  59.5 1.1 %copy.13 = f32[96,4096]{1,0:T(8,128)} copy(f32[96,4096]{1,0:T(8,128)S(1)} %get-tuple-element.5) | data formatting | bytes 3145728
Async XLA Ops:
  2.8 1.1 %copy-start = (bf16[96,4096]{1,0:T(8,128)(2,1)S(1)}, bf16[96,4096]{1,0:T(8,128)(2,1)}, u32[]{:S(2)}) copy-start(bf16[96,4096]{1,0:T(8,128)(2,1)} %sens.1) | copy-start | bytes 2359300
  4.0 0.7 %copy-start.1 = (s32[4096]{0:T(1024)S(1)}, s32[4096]{0:T(1024)}, u32[]{:S(2)}) copy-start(s32[4096]{0:T(1024)} %param.6) | copy-start | bytes 49156
where the time goes:
time: 61.1 us; the launch traced here: 60.7 us
  Pallas kernels  53.7 us (88%)
  local copies, waits for them, and re-layouts  5.69 us (9%)
  between operations  1.29 us (2%)
    pallas_call x1, Pallas kernels, body(): pl.pallas_call(functools.partial(kernel, chunk), out_shape=(out, out), in...  53.7 us
    unnamed x8, local copies, waits for them, and re-layouts  5.69 us

commit v1 on v0

--- a/solution.py
+++ b/solution.py
@@ -23,10 +23,13 @@
     sens,
     owner,
     count,
+    neighbours_in,
+    coupling_in,
+    surface_out,
+    smooth_out,
     neighbours,
     coupling,
-    surface_out,
-    smooth_out,
+    link_sem,
     values,
     owners,
     masked,
@@ -34,8 +37,12 @@
     acc,
     fields,
     weights,
+    table,
+    halo_out,
+    halo_in,
     surface_stage,
     smooth_stage,
+    out_sem,
     load_sem,
     oload_sem,
     send_sem,
@@ -44,10 +51,9 @@
     orecv_sem,
     hsend_sem,
     hrecv_sem,
-    out_sem,
 ):
     columns, faces = sens.shape
-    patches = neighbours.shape[0]
+    patches = neighbours.shape[1]
     span = patches * NODES
     highs = span // LOW
     chunks = faces // chunk
@@ -85,11 +91,15 @@
 
     def halo_copy(side, sweep):
         target = position + 1 if side == 0 else position - 1
-        source = patches if side == 0 else REACH
-        landing = 0 if side == 0 else patches + REACH
+        if sweep == SWEEPS - 1:
+            source = patches if side == 0 else REACH
+            landing = 0 if side == 0 else patches + REACH
+            src, dst = fields.at[sweep, pl.ds(source, REACH)], fields.at[sweep, pl.ds(landing, REACH)]
+        else:
+            src, dst = halo_out.at[side, sweep], halo_in.at[side, sweep]
         return pltpu.make_async_remote_copy(
-            src_ref=fields.at[sweep, pl.ds(source, REACH)],
-            dst_ref=fields.at[sweep, pl.ds(landing, REACH)],
+            src_ref=src,
+            dst_ref=dst,
             send_sem=hsend_sem.at[side, sweep],
             recv_sem=hrecv_sem.at[side, sweep],
             device_id={"surf": target},
@@ -98,6 +108,12 @@
 
     own_owner = pltpu.make_async_copy(owner, owners.at[0], oload_sem)
     own_owner.start()
+    link_copies = (
+        pltpu.make_async_copy(neighbours_in, neighbours, link_sem.at[0]),
+        pltpu.make_async_copy(coupling_in, coupling, link_sem.at[1]),
+    )
+    for link_copy in link_copies:
+        link_copy.start()
     for k in range(chunks):
         local_load(k).start()
 
@@ -139,19 +155,25 @@
         def _(k=k):
             face_copy(1, k).start()
 
-    slots = lax.broadcasted_iota(jnp.int32, neighbours.shape, 0)
+    for link_copy in link_copies:
+        link_copy.wait()
+    slots = lax.broadcasted_iota(jnp.int32, neighbours.shape, 1)
     distance = neighbours[...] - (position * patches + slots)
     links = coupling[...]
-    rows = lax.broadcasted_iota(jnp.int32, (patches, LANES), 0)
-    alive = jnp.where(rows < count[0], 1.0, 0.0).astype(jnp.float32)
-    diagonal = 1.0 + smoothing * (2.0 + jnp.sum(links, axis=1, keepdims=True))
-    share = alive / jnp.broadcast_to(diagonal, alive.shape)
-    weights[NOFF] = share
-    weights[NOFF + 1] = smoothing * share
-    weights[NOFF + 2] = alive
-    for at, offset in enumerate(OFFSETS):
-        total = jnp.sum(jnp.where(distance == offset, links, 0.0), axis=1, keepdims=True)
-        weights[at] = smoothing * share * jnp.broadcast_to(total, alive.shape)
+    along = lax.broadcasted_iota(jnp.int32, (1, patches), 1)
+    alive = jnp.where(along < count[0], 1.0, 0.0).astype(jnp.float32)
+    share = alive / (1.0 + smoothing * (2.0 + jnp.sum(links, axis=0, keepdims=True)))
+    lines = [
+        smoothing * share * jnp.sum(jnp.where(distance == offset, links, 0.0), axis=0, keepdims=True)
+        for offset in OFFSETS
+    ]
+    lines += [share, smoothing * share, alive]
+    table[...] = jnp.zeros_like(table)
+    for at, line in enumerate(lines):
+        table[pl.ds(at, 1), pl.ds(0, patches)] = line
+    turned = jnp.transpose(table[...])
+    for at in range(len(lines)):
+        weights[at] = jnp.broadcast_to(turned[0:patches, at : at + 1], (patches, LANES))
 
     zero_halo = jnp.zeros((REACH, columns, NODES), jnp.float32)
 
@@ -243,22 +265,24 @@
             surface_stage[:, pl.ds(p * NODES, NODES)] = patch
 
     def send_halo(sweep):
-        @pl.when(has_above)
-        def _():
-            halo_copy(0, sweep).start()
-
-        @pl.when(has_below)
-        def _():
-            halo_copy(1, sweep).start()
+        for side, there in ((0, has_above), (1, has_below)):
+
+            @pl.when(there)
+            def _(side=side):
+                if sweep < SWEEPS - 1:
+                    first = patches if side == 0 else REACH
+                    halo_out[side, sweep] = fields[sweep, pl.ds(first, REACH)].astype(jnp.bfloat16)
+                halo_copy(side, sweep).start()
 
     def wait_halo(sweep):
-        @pl.when(has_below)
-        def _():
-            halo_copy(0, sweep).wait_recv()
-
-        @pl.when(has_above)
-        def _():
-            halo_copy(1, sweep).wait_recv()
+        for side, there in ((0, has_below), (1, has_above)):
+
+            @pl.when(there)
+            def _(side=side):
+                halo_copy(side, sweep).wait_recv()
+                if sweep < SWEEPS - 1:
+                    first = 0 if side == 0 else patches + REACH
+                    fields[sweep, pl.ds(first, REACH)] = halo_in[side, sweep].astype(jnp.float32)
 
     ends = REACH * NODES // LOW
     for h in list(range(ends)) + list(range(highs - ends, highs)):
@@ -266,6 +290,7 @@
     send_halo(0)
     for h in range(ends, highs - ends):
         put_surface(h)
+
     surface_copy = pltpu.make_async_copy(surface_stage, surface_out, out_sem.at[0])
     surface_copy.start()
 
@@ -321,19 +346,23 @@
     columns, faces = sensitivity.shape
     patches = neighbours.shape[0]
     span = patches * NODES
-    chunk = min(1024, faces)
+    chunk = min(512, faces)
     chunks = faces // chunk
     highs = span // LOW
-    any_space = pl.BlockSpec(memory_space=pl.ANY)
+    hbm = pl.BlockSpec(memory_space=pltpu.HBM)
     vmem = pl.BlockSpec(memory_space=pltpu.VMEM)
+    links = neighbours.T.shape
     out = jax.ShapeDtypeStruct((columns, span), jnp.float32)
     dma = pltpu.SemaphoreType.DMA
     return pl.pallas_call(
         functools.partial(kernel, chunk),
         out_shape=(out, out),
-        in_specs=[any_space, vmem, pl.BlockSpec(memory_space=pltpu.SMEM), vmem, vmem],
-        out_specs=(any_space, any_space),
+        in_specs=[hbm, hbm, pl.BlockSpec(memory_space=pltpu.SMEM), hbm, hbm],
+        out_specs=(hbm, hbm),
         scratch_shapes=[
+            pltpu.VMEM(links, jnp.int32),
+            pltpu.VMEM(links, jnp.float32),
+            dma((2,)),
             pltpu.VMEM((3, chunks, columns, chunk), jnp.bfloat16),
             pltpu.VMEM((3, faces // LANES, LANES), jnp.int32),
             pltpu.VMEM((highs * columns, chunk), jnp.bfloat16),
@@ -341,8 +370,12 @@
             pltpu.VMEM((highs * columns, LOW), jnp.float32),
             pltpu.VMEM((SWEEPS, patches + 2 * REACH, columns, NODES), jnp.float32),
             pltpu.VMEM((NOFF + 3, patches, LANES), jnp.float32),
+            pltpu.VMEM((16, LANES), jnp.float32),
+            pltpu.VMEM((2, SWEEPS - 1, REACH, columns, NODES), jnp.bfloat16),
+            pltpu.VMEM((2, SWEEPS - 1, REACH, columns, NODES), jnp.bfloat16),
             pltpu.VMEM((columns, span), jnp.float32),
             pltpu.VMEM((columns, span), jnp.float32),
+            dma((2,)),
             dma((chunks,)),
             dma,
             dma((2, chunks)),
@@ -351,12 +384,11 @@
             dma((2,)),
             dma((2, SWEEPS)),
             dma((2, SWEEPS)),
-            dma((2,)),
         ],
         compiler_params=pltpu.CompilerParams(
-            collective_id=0, has_side_effects=True, vmem_limit_bytes=48 * 1024 * 1024
+            collective_id=0, has_side_effects=True, vmem_limit_bytes=63 * 1024 * 1024
         ),
-    )(sensitivity, owner.reshape(faces // LANES, LANES), patch_count, neighbours, coupling)
+    )(sensitivity, owner.reshape(faces // LANES, LANES), patch_count, neighbours.T, coupling.T)
 
 
 def solution(mesh):

time: 61.1 us -> 50.8 us (0.83)
  the two profiles are of different devices: /device:TPU:17 before, /device:TPU:1 now
where the time goes in v1:
time: 50.8 us; the launch traced here: 50.6 us
  Pallas kernels  45.4 us (89%)
  local copies, waits for them, and re-layouts  3.92 us (8%)
  between operations  1.29 us (3%)
    pallas_call x1, Pallas kernels, body(): pl.pallas_call(functools.partial(kernel, chunk), out_shape=(out, out), in...  45.4 us
    unnamed x4, local copies, waits for them, and re-layouts  3.92 us

profile of v1, /device:TPU:1, one launch (start us, length us, event | category | flops | bytes accessed | tf_op | source)
XLA Modules:
  0.0 50.6 jit_solution(12841409445386451720)
XLA Ops:
  1.3 45.4 %shard_map.68 = (f32[96,4096]{1,0:T(8,128)}, f32[96,4096]{1,0:T(8,128)}) custom-call(bf16[96,4096]{1,0:T(8,128)(2,1)} %sens.1, s32[32,128]{1,0:T(8,128)} %bitcast.3, s32[1]{0:T(128)S(6)} %copy.9.count, s32[9,32]{1,0:T(8,128)} %bitcast.4, f32[9,32]{1,0:T(8,128)} %bitcast.5), custom_call_target="tpu_custom_call" | custom-call | tf_op jit(solution)/shard_map/pallas_call | solution.py:357
  46.7 0.0 copy-start
  46.7 2.8 %copy.10 = f32[96,4096]{1,0:T(8,128)} copy(f32[96,4096]{1,0:T(8,128)} %get-tuple-element.4) | data formatting | bytes 3145728
  49.4 0.0 copy-done
  49.4 1.1 %copy.11 = f32[96,4096]{1,0:T(8,128)} copy(f32[96,4096]{1,0:T(8,128)S(1)} %copy-done) | data formatting | bytes 3145728
Async XLA Ops:
  46.7 2.8 %copy-start = (f32[96,4096]{1,0:T(8,128)S(1)}, f32[96,4096]{1,0:T(8,128)}, u32[]{:S(2)}) copy-start(f32[96,4096]{1,0:T(8,128)} %get-tuple-element.5) | copy-start | bytes 4718596

commit v2 on v1

--- a/solution.py
+++ b/solution.py
@@ -12,6 +12,7 @@
 SWEEPS = 4
 LOW = 256
 LANES = 128
+SPLIT = 4
 smoothing = 1.5
 OFFSETS = [d for d in range(-REACH, REACH + 1) if d != 0]
 NOFF = len(OFFSETS)
@@ -342,6 +343,23 @@
                 halo_copy(side, sweep).wait_send()
 
 
+def hand_over(surface, smooth, surface_out, smooth_out, stage, in_sem, out_sem):
+    step = surface.shape[0] // SPLIT
+    fetches, stores = [], []
+    for at, (source, target) in enumerate(((surface, surface_out), (smooth, smooth_out))):
+        for k in range(SPLIT):
+            rows = pl.ds(k * step, step)
+            fetches.append(pltpu.make_async_copy(source.at[rows], stage.at[at, rows], in_sem.at[at, k]))
+            stores.append(pltpu.make_async_copy(stage.at[at, rows], target.at[rows], out_sem.at[at, k]))
+    for fetch in fetches:
+        fetch.start()
+    for fetch, store in zip(fetches, stores):
+        fetch.wait()
+        store.start()
+    for store in stores:
+        store.wait()
+
+
 def body(sensitivity, owner, patch_count, neighbours, coupling):
     columns, faces = sensitivity.shape
     patches = neighbours.shape[0]
@@ -354,7 +372,7 @@
     links = neighbours.T.shape
     out = jax.ShapeDtypeStruct((columns, span), jnp.float32)
     dma = pltpu.SemaphoreType.DMA
-    return pl.pallas_call(
+    outputs = pl.pallas_call(
         functools.partial(kernel, chunk),
         out_shape=(out, out),
         in_specs=[hbm, hbm, pl.BlockSpec(memory_space=pltpu.SMEM), hbm, hbm],
@@ -389,6 +407,14 @@
             collective_id=0, has_side_effects=True, vmem_limit_bytes=63 * 1024 * 1024
         ),
     )(sensitivity, owner.reshape(faces // LANES, LANES), patch_count, neighbours.T, coupling.T)
+    return pl.pallas_call(
+        hand_over,
+        out_shape=(out, out),
+        in_specs=[hbm, hbm],
+        out_specs=(hbm, hbm),
+        scratch_shapes=[pltpu.VMEM((2, columns, span), jnp.float32), dma((2, SPLIT)), dma((2, SPLIT))],
+        compiler_params=pltpu.CompilerParams(vmem_limit_bytes=63 * 1024 * 1024),
+    )(*outputs)
 
 
 def solution(mesh):

time: 50.8 us -> 49.6 us (0.976)
  local copies, waits for them, and re-layouts: 3.92 us -> 0 us
  Pallas kernels: 45.4 us -> 48.2 us
    unnamed x4 -> x0, local copies, waits for them, and re-layouts: 3.92 us -> none
    pallas_call x0 -> x1, Pallas kernels: none -> 2.79 us  [body(): pl.pallas_call(hand_over, out_shape=(out, out), in_specs=[hbm, hbm], out_...]
where the time goes in v2:
time: 49.6 us; the launch traced here: 49.5 us
  Pallas kernels  48.2 us (97%)
  between operations  1.28 us (3%)
    pallas_call x1, Pallas kernels, body(): pl.pallas_call(functools.partial(kernel, chunk), out_shape=(out, out), in...  45.4 us
    pallas_call x1, Pallas kernels, body(): pl.pallas_call(hand_over, out_shape=(out, out), in_specs=[hbm, hbm], out_...  2.79 us

profile of v2, /device:TPU:1, one launch (start us, length us, event | category | flops | bytes accessed | tf_op | source)
XLA Modules:
  0.0 49.5 jit_solution(2022621437485439089)
XLA Ops:
  1.3 45.4 %shard_map.68 = (f32[96,4096]{1,0:T(8,128)}, f32[96,4096]{1,0:T(8,128)}) custom-call(bf16[96,4096]{1,0:T(8,128)(2,1)} %sens.1, s32[32,128]{1,0:T(8,128)} %bitcast.3, s32[1]{0:T(128)S(6)} %copy.7.count, s32[9,32]{1,0:T(8,128)} %bitcast.4, f32[9,32]{1,0:T(8,128)} %bitcast.5), custom_call_target="tpu_custom_call" | custom-call | tf_op jit(solution)/shard_map/pallas_call | solution.py:375
  46.7 2.8 %shard_map.69 = (f32[96,4096]{1,0:T(8,128)}, f32[96,4096]{1,0:T(8,128)}) custom-call(f32[96,4096]{1,0:T(8,128)} %get-tuple-element.4.surface, f32[96,4096]{1,0:T(8,128)} %get-tuple-element.5.smooth), custom_call_target="tpu_custom_call" | custom-call | tf_op jit(solution)/shard_map/pallas_call | solution.py:410
